TPU v7x, 256 devices: a whole 4x4x8 slice. The times are simulated.
256 devices in a mesh: bag: 32 (over x, z), head: 8 (over y, core).
Axes of the slice: x: 4, y: 4, z: 8, core: 2. Of those that a mesh axis runs over, the one named last changes fastest.
Arguments:
- latents: bfloat16 [32, 16, 16, 16, 512], P('bag', 'head'), may hold values from -6 to 6
- frame_counts: int32 [32], P('bag'), may hold values from 8 to 16
- routes: int32 [32768, 1], P('bag'), may hold values from 0 to 31; in each aligned block of 128 rows (0 to 127, 128 to 255, ...) at most 6 rows name the same one
- samples: int32 [32768], P('bag'), may hold values from 0 to 3, as said below
- conv_weight: bfloat16 [27, 512, 128], replicated, may hold values from -0.0546875 to 0.0546875
- embed_weight: bfloat16 [512, 2048], replicated, may hold values from -0.25 to 0.25
- qkv_weight: bfloat16 [3, 2048, 2048], P(None, None, 'head')
Outputs:
- attended: bfloat16 [32768, 2048], P(('bag', 'head'))
Inputs may be any that keep to these rules, and one draw needn't show every extreme that they name: `routes`: in each aligned block of 128 rows (the tokens of one device) no bag is named by more than 6 rows, a bound that some block reaches. `samples`: all tokens of one clip carry the same sample id, and every id occurs in some clip.
All inputs are finite; a program needn't handle non-finite values.
Results may differ from a plain program's by a relative error of at most 0.013.
Values may be sent and summed in bfloat16 or wider, within the bound.
A program may use at most 128 MiB of HBM per device.

v0:
```python
import jax
import jax.numpy as jnp
from jax import lax
from jax.sharding import PartitionSpec as P

HDIM = 64


epsilon = 1e-06
far_below = -1e30


def padded_2(cells, sides, width):
    for axis, dim in sides:
        count = lax.axis_size(axis)
        ends = count - 1
        head = lax.slice_in_dim(cells, 0, width, axis=dim)
        tail = lax.slice_in_dim(cells, cells.shape[dim] - width, cells.shape[dim], axis=dim)
        cells = jnp.concatenate(
            [
                lax.ppermute(tail, axis, [(i, (i + 1) % count) for i in range(ends)]),
                cells,
                lax.ppermute(head, axis, [((i + 1) % count, i) for i in range(ends)]),
            ],
            axis=dim,
        )
    return cells


def patchify(latent_grid):
    frames_in, rows_in, cols_in, chans = latent_grid.shape
    shaped = latent_grid.reshape(frames_in, rows_in // 2, 2, cols_in // 2, 2, chans)
    return shaped.transpose(0, 1, 3, 2, 4, 5).reshape(
        frames_in * (rows_in // 2) * (cols_in // 2), 4 * chans
    )


def project(embedded, qkv_weight):
    widened = embedded.astype(jnp.float32)
    normed = (
        widened * lax.rsqrt(jnp.mean(widened * widened, axis=-1, keepdims=True) + epsilon)
    ).astype(jnp.bfloat16)
    return jnp.einsum("rd,mdc->rmc", normed, qkv_weight, preferred_element_type=jnp.float32).astype(
        jnp.bfloat16
    )


def convolve(padded, conv_weight, frame_live, frames_dev, side_rows, side_cols):
    depth_in = padded.shape[3]
    accumulated = jnp.zeros((frames_dev * side_rows * side_cols, conv_weight.shape[2]), jnp.float32)
    for offset_t in range(3):
        for offset_h in range(3):
            for offset_w in range(3):
                window = padded[
                    offset_t : offset_t + frames_dev,
                    offset_h : offset_h + side_rows,
                    offset_w : offset_w + side_cols,
                ]
                accumulated = accumulated + jnp.dot(
                    window.reshape(-1, depth_in),
                    conv_weight[9 * offset_t + 3 * offset_h + offset_w],
                    preferred_element_type=jnp.float32,
                )
    shaped = accumulated.reshape(frames_dev, side_rows, side_cols, -1)
    shaped = shaped * frame_live[:, None, None, None].astype(jnp.float32)
    return patchify(shaped.astype(jnp.bfloat16))


def shards(latents, frame_counts, routes, samples, conv_weight, embed_weight, qkv_weight):
    frames_dev = latents.shape[1]
    side_rows = latents.shape[2]
    side_cols = latents.shape[3]
    heads_dev = lax.axis_size("head")
    bags = lax.axis_size("bag")
    place = lax.axis_index("head")
    frame_count = frame_counts[0]
    frame_ids = place * frames_dev + jnp.arange(frames_dev, dtype=jnp.int32)
    frame_live = frame_ids < frame_count
    masked = latents[0] * frame_live[:, None, None, None].astype(jnp.bfloat16)
    padded = padded_2(masked, (("head", 0),), 1)
    padded = jnp.pad(padded, ((0, 0), (1, 1), (1, 1), (0, 0)))
    patches = convolve(padded, conv_weight, frame_live, frames_dev, side_rows, side_cols)
    tok_dev = patches.shape[0]
    embedded_rows = jnp.dot(
        lax.all_gather(patches, "head", axis=0, tiled=True),
        embed_weight,
        preferred_element_type=jnp.float32,
    ).astype(jnp.bfloat16)
    qkv_all = project(embedded_rows, qkv_weight)
    local_width = qkv_all.shape[2]
    route_rows = routes[:, 0].reshape(heads_dev, tok_dev)
    per_frame = tok_dev // frames_dev
    token_frame = (
        jnp.arange(heads_dev, dtype=jnp.int32)[:, None] * frames_dev
        + (jnp.arange(tok_dev, dtype=jnp.int32) // per_frame)[None, :]
    )
    token_live = token_frame < frame_count
    bag_ids = jnp.arange(bags, dtype=jnp.int32)
    onehot = (route_rows[:, :, None] == bag_ids[None, None, :]).astype(jnp.int32)
    slot_rank = jnp.sum((jnp.cumsum(onehot, axis=1) - onehot) * onehot, axis=2)
    capacity = 3 * tok_dev // (2 * bags)
    matches = (route_rows[None, :, None, :] == bag_ids[:, None, None, None]) & (
        slot_rank[None, :, None, :] == jnp.arange(capacity, dtype=jnp.int32)[None, None, :, None]
    )
    positions = jnp.arange(tok_dev, dtype=jnp.int32)
    slot_token = jnp.sum(jnp.where(matches, positions[None, None, None, :], 0), axis=3)
    filled = jnp.any(matches, axis=3)
    flat_index = jnp.arange(heads_dev, dtype=jnp.int32)[None, :, None] * tok_dev + slot_token
    slot_live = filled & token_live.reshape(-1)[flat_index]
    slot_labels = jnp.where(slot_live, samples[flat_index], -1).reshape(bags, heads_dev * capacity)
    outgoing = jnp.take(qkv_all, flat_index.reshape(-1), axis=0).reshape(
        bags, heads_dev * capacity, 3, local_width
    )
    incoming, incoming_labels = (
        lax.all_to_all(outgoing, "bag", split_axis=0, concat_axis=0, tiled=True),
        lax.all_to_all(slot_labels, "bag", split_axis=0, concat_axis=0, tiled=True),
    )
    count_slots = bags * heads_dev * capacity
    heads_here = local_width // HDIM
    slot_rows = incoming.reshape(count_slots, 3, local_width)
    labels_all = incoming_labels.reshape(count_slots)
    key_rows = slot_rows[:, 1].reshape(count_slots, heads_here, HDIM)
    value_rows = slot_rows[:, 2].reshape(count_slots, heads_here, HDIM)
    block_count = max(1, count_slots // 512)
    block_size = count_slots // block_count
    key_ok = labels_all >= 0

    def attend(operands):
        query_block, label_block = operands
        scores = jnp.einsum(
            "qhd,khd->hqk", query_block, key_rows, preferred_element_type=jnp.float32
        ) * HDIM ** (-0.5)
        admissible = (labels_all[None, :] == label_block[:, None]) & key_ok[None, :]
        scores = jnp.where(admissible[None, :, :], scores, far_below)
        shifted = jnp.exp(scores - jnp.max(scores, axis=-1, keepdims=True))
        weights = (shifted / jnp.sum(shifted, axis=-1, keepdims=True)).astype(jnp.bfloat16)
        mixed = jnp.einsum("hqk,khd->qhd", weights, value_rows, preferred_element_type=jnp.float32)
        return mixed.astype(jnp.bfloat16).reshape(block_size, local_width)

    query_blocks = slot_rows[:, 0].reshape(block_count, block_size, heads_here, HDIM)
    outputs = lax.map(attend, (query_blocks, labels_all.reshape(block_count, block_size)))
    outputs = outputs.reshape(bags, heads_dev, capacity, local_width)
    own_route = jnp.take(route_rows, place, axis=0)
    own_rank = jnp.take(slot_rank, place, axis=0)
    own_live = jnp.take(token_live, place, axis=0)
    returned = lax.all_to_all(
        lax.all_to_all(outputs, "bag", split_axis=0, concat_axis=0, tiled=True),
        "head",
        split_axis=1,
        concat_axis=3,
        tiled=True,
    )
    home_table = returned.reshape(bags * capacity, local_width * heads_dev)
    picked = jnp.take(home_table, own_route * capacity + own_rank, axis=0)
    return jnp.where(own_live[:, None], picked, jnp.zeros((), jnp.bfloat16))


def solution(mesh):
    placed = (
        P("bag", "head", None, None, None),
        P("bag"),
        P("bag", None),
        P("bag"),
        P(),
        P(),
        P(None, None, "head"),
    )
    return jax.shard_map(
        shards, mesh=mesh, in_specs=placed, out_specs=P(("bag", "head"), None), check_vma=False
    )
```

profile of v0, /device:TPU:1, one launch (start us, length us, event | category | flops | bytes accessed | tf_op | source)
XLA Modules:
  0.0 322.4 jit_solution(2346358537378281575)
XLA Ops:
  7.4 1.3 bitcast_multiply_fusion
  8.7 0.8 copy-done.3
  9.4 0.8 fusion.146
  10.3 4.6 %collective-permute-start = (bf16[1,16,16,512]{3,2,1,0:T(8,128)(2,1)}, bf16[1,16,16,512]{3,2,1,0:T(8,128)(2,1)}, u32[]{:S(2)}, u32[]{:S(2)}) collective-permute-start(bf16[1,16,16,512]{3,2,1,0:T(8,128)(2,1)} %get-tuple-element.176), channel_id=1, source_target_pairs={{0,1},{1,2},{2,3},{3,4},{4,5},{5,6},{6,7},{8,9},{9,10},{10,11},{11... | collective-permute-start | bytes 786440 | tf_op jit(solution)/shard_map/ppermute | solution.py:21
  14.9 2.5 collective-permute-start.1
  17.4 0.7 iota_compare_fusion.6
  18.1 0.8 copy.112
  18.9 1.9 broadcast_multiply_fusion
  20.9 2.5 select_reduce_fusion
  23.4 0.6 copy-done.7
  24.0 3.3 %fusion.52 = s32[32,8,6]{1,2,0:T(8,128)S(1)} fusion(pred[8,6,128]{2,0,1:T(8,128)(4,1)S(1)} %iota_compare_fusion.7, pred[32,8,128]{2,1,0:T(8,128)(4,1)S(1)} %iota_compare_fusion.6), kind=kLoop, calls=%fused_computation.73 | loop fusion | flops 588288 | bytes 45056 | tf_op jit(solution)/shard_map/reduce_sum | solution.py:106
  27.3 1.4 fusion.84
  28.7 2.3 select_maximum_fusion
  31.1 0.6 fusion.145
  31.7 2.7 fusion.144
  34.4 1.1 pad_maximum_fusion.1
  43.3 0.7 fusion.57
  44.1 0.7 compare_select_fusion
  44.8 1.2 copy.114
  46.2 0.5 copy-done.10
  46.7 9.4 %gather_fusion = pred[1536]{0:T(1024)(128)(4,1)S(1)} fusion(pred[1024]{0:T(1024)(128)(4,1)S(1)} %fusion.179, s32[2048]{0:T(1024)S(1)} %pad_clamp_fusion.1), kind=kCustom, calls=%fused_computation | custom fusion | bytes 9216 | tf_op jit(solution)/shard_map/gather | solution.py:109
  56.2 5.9 %gather_fusion.1 = s32[1536]{0:T(1024)S(1)} fusion(s32[1024]{0:T(1024)S(1)} %copy-done.2, s32[2048]{0:T(1024)S(1)} %pad_clamp_fusion.1), kind=kCustom, calls=%fused_computation.1 | custom fusion | bytes 18432 | tf_op jit(solution)/shard_map/gather | solution.py:110
  62.6 0.9 copy.116
  63.5 3.4 %and_reduce_fusion = pred[32,8,6]{1,2,0:T(8,128)(4,1)S(1)} fusion(pred[8,6,128]{2,0,1:T(8,128)(4,1)S(1)} %iota_compare_fusion.7, pred[32,8,128]{2,1,0:T(8,128)(4,1)S(1)} %iota_compare_fusion.6), kind=kLoop, calls=%fused_computation.72 | loop fusion | flops 391680 | bytes 40448 | tf_op jit(solution)/shard_map/reduce_or | solution.py:107
  66.9 0.9 and_select_fusion.1
  68.0 0.7 copy.118
  68.7 10.6 %all-to-all-start = ((s32[32,1,48]{2,1,0:T(1,128)}), s32[32,1,48]{2,1,0:T(1,128)S(1)}, u32[]{:S(2)}, u32[]{:S(2)}) async-start(s32[32,1,48]{2,1,0:T(1,128)} %copy.118), calls=%async_computation | async-start | bytes 32768 | tf_op jit(solution)/shard_map/all_to_all | solution.py:116
  80.2 4.3 %fusion.13 = (f32[1024]{0:T(1024)S(1)}, bf16[1024,2048]{1,0:T(8,128)(2,1)S(1)}) fusion(bf16[1024,512]{1,0:T(8,128)(2,1)} %all-gather.2.cloned.1.call-done, bf16[512,2048]{1,0:T(8,128)(2,1)} %param.16), kind=kOutput, calls=%fused_computation.25 | convolution fusion | flops 2155871232 | bytes 7344128 | tf_op jit(solution)/shard_map/dot_general | solution.py:84
  84.5 3.5 %fusion.25 = bf16[1024,3,256]{2,0,1:T(8,128)(2,1)S(1)} fusion(bf16[3,2048,256]{2,1,0:T(8,128)(2,1)S(1)} %copy-done, bf16[1024,2048]{1,0:T(8,128)(2,1)S(1)} %get-tuple-element.179, f32[1024]{0:T(1024)S(1)} %add_rsqrt_fusion), kind=kOutput, calls=%fused_computation.44 | convolution fusion | flops 3228303360 | bytes 8916992 | tf_op jit(solution)/shard_map/rd,mdc->rmc/dot_general | solution.py:43
  88.0 1.4 copy.124
  89.4 6.2 %gather_fusion.2 = bf16[1536,3,256]{2,1,0:T(4,128)(2,1)} fusion(bf16[1024,3,256]{2,1,0:T(4,128)(2,1)S(1)} %copy.124, s32[2048]{0:T(1024)S(1)} %pad_clamp_fusion), kind=kCustom, calls=%fused_computation.2 | custom fusion | bytes 4724736 | tf_op jit(solution)/shard_map/jit(_take)/gather | solution.py:111
  95.5 3.4 %copy_select_fusion = bf16[32,48,3,256]{3,1,2,0:T(8,128)(2,1)} fusion(bf16[32,48,3,256]{3,2,1,0:T(4,128)(2,1)} %bitcast.219, pred[32,48]{1,0:T(8,128)(4,1)S(1)} %compare_and_fusion.1), kind=kLoop, calls=%fused_computation.38 | loop fusion | flops 1179648 | bytes 4720128 | tf_op jit(solution)/shard_map/jit(_take)/select_n | solution.py:111
  98.9 9.3 %all-to-all-start.1 = ((bf16[32,48,3,256]{3,1,2,0:T(8,128)(2,1)}), bf16[32,48,3,256]{3,1,2,0:T(8,128)(2,1)S(1)}, u32[]{:S(2)}, u32[]{:S(2)}) async-start(bf16[32,48,3,256]{3,1,2,0:T(8,128)(2,1)} %copy_select_fusion), calls=%async_computation.1 | async-start | bytes 4718592 | tf_op jit(solution)/shard_map/all_to_all | solution.py:115
  108.4 0.6 broadcast.339
  109.0 0.7 reduce.9
  109.8 54.1 %all-to-all-done.1 = bf16[32,48,3,256]{3,1,2,0:T(8,128)(2,1)S(1)} async-done(((bf16[32,48,3,256]{3,1,2,0:T(8,128)(2,1)}), bf16[32,48,3,256]{3,1,2,0:T(8,128)(2,1)S(1)}, u32[]{:S(2)}, u32[]{:S(2)}) %all-to-all-start.1) | async-done | bytes 2359328 | tf_op jit(solution)/shard_map/all_to_all | solution.py:115
  164.2 1.2 copy.129
  165.7 0.7 reshape.476
  166.4 0.9 copy.130
  167.3 91.5 %while.13 = (s32[]{:T(128)}, bf16[3,512,256]{2,1,0:T(8,128)(2,1)}, s32[32,48]{1,0:T(8,128)}, s32[3,512]{1,0:T(4,128)S(1)}, pred[1536]{0:T(1024)(128)(4,1)S(1)}, ...) while((s32[]{:T(128)}, bf16[3,512,256]{2,1,0:T(8,128)(2,1)}, ...), condition=%wide.wide.region_8.10_spmd, body=%wide.wide.region_5.9_spmd.sunk | while | flops 832177664 | bytes 58226324 | solution.py:141
  167.3 0.6 compare_and_fusion.5
  167.9 6.4 %fusion.195 = f32[4,512,1536]{2,1,0:T(8,128)} fusion(bf16[1536,4,64]{0,2,1:T(8,128)(2,1)S(1)} %get-tuple-element.301, bf16[3,512,4,64]{1,3,2,0:T(8,128)(2,1)S(1)} %get-tuple-element.300, s32[]{:T(128)S(6)} %copy.151), kind=kOutput, calls=%fused_computation.15.clone.clone.1 | convolution fusion | flops 402653184 | bytes 13631492 | tf_op jit(solution)/shard_map/while/body/eval_jaxpr/qhd,khd->hqk/dot_general | solution.py:130
  174.3 15.9 %fusion.196 = (f32[4,512]{1,0:T(4,128)S(1)}, f32[4,512,1536]{2,1,0:T(8,128)}) fusion(f32[4,512,1536]{2,1,0:T(8,128)} %fusion.195, pred[512,1536]{1,0:T(8,128)(4,1)S(1)} %compare_and_fusion.5), kind=kOutput, calls=%fused_computation.200.clone.clone.1 | output fusion | flops 18875904 | bytes 25960448 | tf_op jit(solution)/shard_map/while/body/eval_jaxpr/sub | solution.py:135
  190.3 6.7 %fusion.197 = bf16[4,512,64]{1,2,0:T(8,128)(2,1)S(1)} fusion(bf16[1536,4,64]{0,2,1:T(8,128)(2,1)S(1)} %copy-done.6, f32[4,512,1536]{2,1,0:T(8,128)} %get-tuple-element.273, f32[4,512]{1,0:T(4,128)S(1)} %get-tuple-element.274), kind=kOutput, calls=%fused_computation.14.clone.clone.1 | convolution fusion | flops 409075712 | bytes 13639680 | tf_op jit(solution)/shard_map/while/body/eval_jaxpr/hqk,khd->qhd/dot_general | solution.py:137
  197.1 0.8 constant_dynamic-update-slice_fusion.3
  197.9 0.6 compare_and_fusion.5
  198.4 6.4 %fusion.195 = f32[4,512,1536]{2,1,0:T(8,128)} fusion(bf16[1536,4,64]{0,2,1:T(8,128)(2,1)S(1)} %get-tuple-element.301, bf16[3,512,4,64]{1,3,2,0:T(8,128)(2,1)S(1)} %get-tuple-element.300, s32[]{:T(128)S(6)} %copy.151), kind=kOutput, calls=%fused_computation.15.clone.clone.1 | convolution fusion | flops 402653184 | bytes 13631492 | tf_op jit(solution)/shard_map/while/body/eval_jaxpr/qhd,khd->hqk/dot_general | solution.py:130
  204.8 15.9 %fusion.196 = (f32[4,512]{1,0:T(4,128)S(1)}, f32[4,512,1536]{2,1,0:T(8,128)}) fusion(f32[4,512,1536]{2,1,0:T(8,128)} %fusion.195, pred[512,1536]{1,0:T(8,128)(4,1)S(1)} %compare_and_fusion.5), kind=kOutput, calls=%fused_computation.200.clone.clone.1 | output fusion | flops 18875904 | bytes 25960448 | tf_op jit(solution)/shard_map/while/body/eval_jaxpr/sub | solution.py:135
  220.8 6.7 %fusion.197 = bf16[4,512,64]{1,2,0:T(8,128)(2,1)S(1)} fusion(bf16[1536,4,64]{0,2,1:T(8,128)(2,1)S(1)} %copy-done.6, f32[4,512,1536]{2,1,0:T(8,128)} %get-tuple-element.273, f32[4,512]{1,0:T(4,128)S(1)} %get-tuple-element.274), kind=kOutput, calls=%fused_computation.14.clone.clone.1 | convolution fusion | flops 409075712 | bytes 13639680 | tf_op jit(solution)/shard_map/while/body/eval_jaxpr/hqk,khd->qhd/dot_general | solution.py:137
  227.6 0.7 constant_dynamic-update-slice_fusion.3
  228.3 0.6 compare_and_fusion.5
  228.9 6.4 %fusion.195 = f32[4,512,1536]{2,1,0:T(8,128)} fusion(bf16[1536,4,64]{0,2,1:T(8,128)(2,1)S(1)} %get-tuple-element.301, bf16[3,512,4,64]{1,3,2,0:T(8,128)(2,1)S(1)} %get-tuple-element.300, s32[]{:T(128)S(6)} %copy.151), kind=kOutput, calls=%fused_computation.15.clone.clone.1 | convolution fusion | flops 402653184 | bytes 13631492 | tf_op jit(solution)/shard_map/while/body/eval_jaxpr/qhd,khd->hqk/dot_general | solution.py:130
  235.3 15.9 %fusion.196 = (f32[4,512]{1,0:T(4,128)S(1)}, f32[4,512,1536]{2,1,0:T(8,128)}) fusion(f32[4,512,1536]{2,1,0:T(8,128)} %fusion.195, pred[512,1536]{1,0:T(8,128)(4,1)S(1)} %compare_and_fusion.5), kind=kOutput, calls=%fused_computation.200.clone.clone.1 | output fusion | flops 18875904 | bytes 25960448 | tf_op jit(solution)/shard_map/while/body/eval_jaxpr/sub | solution.py:135
  251.3 6.7 %fusion.197 = bf16[4,512,64]{1,2,0:T(8,128)(2,1)S(1)} fusion(bf16[1536,4,64]{0,2,1:T(8,128)(2,1)S(1)} %copy-done.6, f32[4,512,1536]{2,1,0:T(8,128)} %get-tuple-element.273, f32[4,512]{1,0:T(4,128)S(1)} %get-tuple-element.274), kind=kOutput, calls=%fused_computation.14.clone.clone.1 | convolution fusion | flops 409075712 | bytes 13639680 | tf_op jit(solution)/shard_map/while/body/eval_jaxpr/hqk,khd->qhd/dot_general | solution.py:137
  258.1 0.7 constant_dynamic-update-slice_fusion.3
  258.8 1.3 reshape.363
  260.4 26.1 %all_to_all.34 = bf16[32,8,6,256]{3,1,2,0:T(8,128)(2,1)S(1)} all-to-all(bf16[32,8,6,256]{3,1,2,0:T(8,128)(2,1)S(1)} %copy.132), channel_id=1, replica_groups=mesh['bag'=32,'head'=8] {'bag'}, dimensions={0} | all-to-all | bytes 1572864 | tf_op jit(solution)/shard_map/all_to_all | solution.py:147
  286.5 1.1 copy.133
  287.7 8.2 %all-to-all-start.3 = ((bf16[32,8,6,256]{3,0,2,1:T(8,128)(2,1)}), bf16[32,8,6,256]{3,0,2,1:T(8,128)(2,1)S(1)}, u32[]{:S(2)}, u32[]{:S(2)}) async-start(bf16[32,8,6,256]{3,0,2,1:T(8,128)(2,1)} %copy.133), calls=%async_computation.3 | async-start | bytes 1572864 | tf_op jit(solution)/shard_map/all_to_all | solution.py:146
  296.2 0.7 compare_and_fusion.2
  296.9 11.3 %all-to-all-done.3 = bf16[32,8,6,256]{3,0,2,1:T(8,128)(2,1)S(1)} async-done(((bf16[32,8,6,256]{3,0,2,1:T(8,128)(2,1)}), bf16[32,8,6,256]{3,0,2,1:T(8,128)(2,1)S(1)}, u32[]{:S(2)}, u32[]{:S(2)}) %all-to-all-start.3) | async-done | bytes 786464 | tf_op jit(solution)/shard_map/all_to_all | solution.py:146
  308.6 1.1 copy.140
  309.7 3.6 %gather_fusion.3 = bf16[128,2048]{1,0:T(8,128)(2,1)} fusion(bf16[192,2048]{1,0:T(8,128)(2,1)} %bitcast.218, s32[1024]{0:T(1024)S(1)} %pad_clamp_fusion.2), kind=kCustom, calls=%fused_computation.3 | custom fusion | bytes 1049088 | tf_op jit(solution)/shard_map/jit(_take)/gather | solution.py:154
  313.3 2.0 select_select_fusion
  (108 shorter events, 11.9 us)
Async XLA Ops:
  6.5 78.0 %copy-start = (bf16[3,2048,256]{2,1,0:T(8,128)(2,1)S(1)}, bf16[3,2048,256]{2,1,0:T(8,128)(2,1)}, u32[]{:S(2)}) copy-start(bf16[3,2048,256]{2,1,0:T(8,128)(2,1)} %param.17) | copy-start | bytes 9437188
  6.5 73.6 %all-gather.2.cloned.1.call-start = ((), (), s32[]{:S(2)}) async-start(), calls=%async_computation.4 | async-start | bytes 1179648 | tf_op jit(solution)/shard_map/all_gather | solution.py:85
  8.6 0.8 copy-start.3
  10.3 18.4 %collective-permute-start = (bf16[1,16,16,512]{3,2,1,0:T(8,128)(2,1)}, bf16[1,16,16,512]{3,2,1,0:T(8,128)(2,1)}, u32[]{:S(2)}, u32[]{:S(2)}) collective-permute-start(bf16[1,16,16,512]{3,2,1,0:T(8,128)(2,1)} %get-tuple-element.176), channel_id=1, source_target_pairs={{0,1},{1,2},{2,3},{3,4},{4,5},{5,6},{6,7},{8,9},{9,10},{10,11},{11... | collective-permute-start | bytes 786440 | tf_op jit(solution)/shard_map/ppermute | solution.py:21
  14.9 13.8 %collective-permute-start.1 = (bf16[1,16,16,512]{3,2,1,0:T(8,128)(2,1)}, bf16[1,16,16,512]{3,2,1,0:T(8,128)(2,1)}, u32[]{:S(2)}, u32[]{:S(2)}) collective-permute-start(bf16[1,16,16,512]{3,2,1,0:T(8,128)(2,1)} %get-tuple-element.177), channel_id=1, source_target_pairs={{1,0},{2,1},{3,2},{4,3},{5,4},{6,5},{7,6},{9,8},{10,9},{11,10},{12... | collective-permute-start | bytes 786440 | tf_op jit(solution)/shard_map/ppermute | solution.py:23
  23.4 0.6 copy-start.7
  31.6 2.7 copy-start.4
  31.7 3.9 %copy-start.5 = (bf16[27,512,128]{2,1,0:T(8,128)(2,1)S(1)}, bf16[27,512,128]{2,1,0:T(8,128)(2,1)}, u32[]{:S(2)}) copy-start(bf16[27,512,128]{2,1,0:T(8,128)(2,1)} %param.15) | copy-start | bytes 10616836
  46.1 0.6 copy-start.10
  46.1 10.0 %copy-start.12 = (s32[128]{0:T(128)}, s32[128]{0:T(128)S(1)}, u32[]{:S(2)}) copy-start(s32[128]{0:T(128)S(1)} %and_select_fusion.2) | copy-start | bytes 1540
  46.7 9.5 %copy-start.2 = (s32[1024]{0:T(1024)S(1)}, s32[1024]{0:T(1024)}, u32[]{:S(2)}) copy-start(s32[1024]{0:T(1024)} %param.14) | copy-start | bytes 12292
  68.7 30.3 %all-to-all-start = ((s32[32,1,48]{2,1,0:T(1,128)}), s32[32,1,48]{2,1,0:T(1,128)S(1)}, u32[]{:S(2)}, u32[]{:S(2)}) async-start(s32[32,1,48]{2,1,0:T(1,128)} %copy.118), calls=%async_computation | async-start | bytes 32768 | tf_op jit(solution)/shard_map/all_to_all | solution.py:116
  98.9 65.1 %copy-start.9 = (s32[32,1,48]{2,1,0:T(1,128)}, s32[32,1,48]{2,1,0:T(1,128)S(1)}, u32[]{:S(2)}) copy-start(s32[32,1,48]{2,1,0:T(1,128)S(1)} %all-to-all-done) | copy-start | bytes 18436
  98.9 64.9 %all-to-all-start.1 = ((bf16[32,48,3,256]{3,1,2,0:T(8,128)(2,1)}), bf16[32,48,3,256]{3,1,2,0:T(8,128)(2,1)S(1)}, u32[]{:S(2)}, u32[]{:S(2)}) async-start(bf16[32,48,3,256]{3,1,2,0:T(8,128)(2,1)} %copy_select_fusion), calls=%async_computation.1 | async-start | bytes 4718592 | tf_op jit(solution)/shard_map/all_to_all | solution.py:115
  174.3 16.0 %copy-start.6 = (bf16[1536,4,64]{0,2,1:T(8,128)(2,1)S(1)}, bf16[1536,4,64]{0,2,1:T(8,128)(2,1)}, u32[]{:S(2)}) copy-start(bf16[1536,4,64]{0,2,1:T(8,128)(2,1)} %get-tuple-element.302) | copy-start | bytes 2359300 | tf_op jit(solution)/shard_map/while
  204.8 16.0 %copy-start.6 = (bf16[1536,4,64]{0,2,1:T(8,128)(2,1)S(1)}, bf16[1536,4,64]{0,2,1:T(8,128)(2,1)}, u32[]{:S(2)}) copy-start(bf16[1536,4,64]{0,2,1:T(8,128)(2,1)} %get-tuple-element.302) | copy-start | bytes 2359300 | tf_op jit(solution)/shard_map/while
  235.3 16.0 %copy-start.6 = (bf16[1536,4,64]{0,2,1:T(8,128)(2,1)S(1)}, bf16[1536,4,64]{0,2,1:T(8,128)(2,1)}, u32[]{:S(2)}) copy-start(bf16[1536,4,64]{0,2,1:T(8,128)(2,1)} %get-tuple-element.302) | copy-start | bytes 2359300 | tf_op jit(solution)/shard_map/while
  260.1 35.7 %copy-start.8 = (s32[8,128]{0,1:T(8,128)S(1)}, s32[8,128]{0,1:T(8,128)}, u32[]{:S(2)}) copy-start(s32[8,128]{0,1:T(8,128)} %copy-done.7) | copy-start | bytes 12292
  260.1 35.9 %copy-start.11 = (s32[8]{0:T(128)S(1)}, s32[8]{0:T(128)}, u32[]{:S(2)}) copy-start(s32[8]{0:T(128)} %copy-done.10) | copy-start | bytes 100
  260.2 35.9 %copy-start.13 = (s32[128]{0:T(128)S(1)}, s32[128]{0:T(128)}, u32[]{:S(2)}) copy-start(s32[128]{0:T(128)} %copy-done.12) | copy-start | bytes 1540
  287.7 20.5 %all-to-all-start.3 = ((bf16[32,8,6,256]{3,0,2,1:T(8,128)(2,1)}), bf16[32,8,6,256]{3,0,2,1:T(8,128)(2,1)S(1)}, u32[]{:S(2)}, u32[]{:S(2)}) async-start(bf16[32,8,6,256]{3,0,2,1:T(8,128)(2,1)} %copy.133), calls=%async_computation.3 | async-start | bytes 1572864 | tf_op jit(solution)/shard_map/all_to_all | solution.py:146
  308.6 6.7 %copy-start.1 = (bf16[3,2048,256]{2,1,0:T(8,128)(2,1)S(1)}, bf16[3,2048,256]{2,1,0:T(8,128)(2,1)}, u32[]{:S(2)}) copy-start(bf16[3,2048,256]{2,1,0:T(8,128)(2,1)} %param.17) | copy-start | bytes 9437188
Sparse Core Ops, SparseCore 0:
  44.2 28.5 all-gather.1
where the time goes:
time: 328 us; the launch traced here: 322 us
  other arithmetic  75.9 us (23%)
  waiting for transfers between devices  65.4 us (20%)
  matrix products  56 us (17%)
  local copies, waits for them, and re-layouts  48.6 us (15%)
  starting transfers between devices  35.2 us (11%)
  blocking collectives  26.1 us (8%)
  between operations  15.1 us (5%)
    all_to_all x1, waiting for transfers between devices, shards(): lax.all_to_all(outgoing, 'bag', split_axis=0, concat_axis=0, tiled=True)  54.1 us
    sub x3, other arithmetic, attend(): shifted = jnp.exp(scores - jnp.max(scores, axis=-1, keepdims=True))  47.8 us
    all_to_all x1, blocking collectives, shards(): lax.all_to_all(outputs, 'bag', split_axis=0, concat_axis=0, tiled=True)  26.1 us
    dot_general x3, matrix products, attend(): jnp.einsum('hqk,khd->qhd', weights, value_rows, preferred_element_type=jn...  20 us
    dot_general x3, matrix products, attend(): jnp.einsum('qhd,khd->hqk', query_block, key_rows, preferred_element_type=...  19.2 us
    all_to_all x1, waiting for transfers between devices, shards(): lax.all_to_all(lax.all_to_all(outputs, 'bag', split_axis=0, concat_axis=0...  11.3 us
    all_to_all x1, starting transfers between devices, shards(): lax.all_to_all(slot_labels, 'bag', split_axis=0, concat_axis=0, tiled=True)  10.6 us
    gather x3, local copies, waits for them, and re-layouts, shards(): slot_live = filled & token_live.reshape(-1)[flat_index]  9.89 us
  transfers between devices with their start and end apart: 6, of which 2 were waited for; matrix products, arithmetic and copies ran while one was open for 18% of the time, Pallas kernels for 0%

commit v1 on v0

v1 whole, which is shorter than its diff:
```python
import jax
import jax.numpy as jnp
from jax import lax
from jax.experimental import pallas as pl
from jax.experimental.pallas import tpu as pltpu
from jax.sharding import PartitionSpec as P

BAGS = 32
HEAD_DEVS = 8
CORES = 2
TOK = 128
CAP = 6
MSG = 32
ROWS = BAGS * CAP
SLOTS = HEAD_DEVS * ROWS
PER_BAG = HEAD_DEVS * CAP
FRAMES_DEV = 2
CELLS = 256
CIN = 512
COUT = 128
D = 2048
WIDTH = 256
HDIM = 64
QTILE = 128
TILE = 256
SORTED = SLOTS + 64 + TILE
epsilon = 1e-06
far_below = -1e30

MESH = pl.DeviceIdType.MESH
bf16 = jnp.bfloat16
f32 = jnp.float32
i32 = jnp.int32


def iota(shape, dim):
    return lax.broadcasted_iota(i32, shape, dim)


def dot(a, b):
    return jnp.dot(a, b, preferred_element_type=f32)


def greet(bag, head):
    barrier = pltpu.get_barrier_semaphore()

    def along_bag(step, carry):
        pl.semaphore_signal(
            barrier, inc=1, device_id=(lax.rem(bag + step, BAGS), head), device_id_type=MESH
        )
        return carry

    lax.fori_loop(1, BAGS, along_bag, 0)

    def along_head(step, carry):
        pl.semaphore_signal(
            barrier, inc=1, device_id=(bag, lax.rem(head + step, HEAD_DEVS)), device_id_type=MESH
        )
        return carry

    lax.fori_loop(1, HEAD_DEVS, along_head, 0)
    pl.semaphore_wait(barrier, BAGS + HEAD_DEVS - 2)


def front_kernel(
    count_ref,
    routes_ref,
    samples_ref,
    latents_ref,
    conv_ref,
    rows_ref,
    pos_ref,
    plan_ref,
    taps,
    frames,
    sums,
    grid,
    scatter,
    outbox,
    inbox,
    unpack,
    own_rows,
    load_sem,
    tap_sem,
    halo_send,
    halo_recv,
    bag_send,
    bag_recv,
    local_sem,
    head_send,
    head_recv,
):
    bag = lax.axis_index("bag")
    head = lax.axis_index("head")
    core = lax.rem(head, CORES)
    chip = lax.div(head, CORES)
    count = count_ref[0]

    loads = [
        pltpu.make_async_copy(latents_ref.at[f], frames.at[f + 1], load_sem.at[f])
        for f in range(FRAMES_DEV)
    ]
    for load in loads:
        load.start()
    for a in (1, 0, 2):
        for be in range(9):
            pltpu.make_async_copy(
                conv_ref.at[9 * a + be], taps.at[a, :, pl.ds(be * COUT, COUT)], tap_sem.at[a]
            ).start()

    @pl.when(head == 0)
    def _():
        frames[0] = jnp.zeros((CELLS, CIN), bf16)

    @pl.when(head == HEAD_DEVS - 1)
    def _():
        frames[3] = jnp.zeros((CELLS, CIN), bf16)

    greet(bag, head)

    to_right = pltpu.make_async_remote_copy(
        src_ref=latents_ref.at[FRAMES_DEV - 1],
        dst_ref=frames.at[0],
        send_sem=halo_send.at[0],
        recv_sem=halo_recv.at[0],
        device_id=(bag, lax.rem(head + 1, HEAD_DEVS)),
        device_id_type=MESH,
    )
    to_left = pltpu.make_async_remote_copy(
        src_ref=latents_ref.at[0],
        dst_ref=frames.at[3],
        send_sem=halo_send.at[1],
        recv_sem=halo_recv.at[1],
        device_id=(bag, lax.rem(head + HEAD_DEVS - 1, HEAD_DEVS)),
        device_id_type=MESH,
    )

    @pl.when(head < HEAD_DEVS - 1)
    def _():
        to_right.start()

    @pl.when(head > 0)
    def _():
        to_left.start()

    lane = iota((1, TOK), 1)
    bag_row = iota((BAGS, TOK), 0)
    half = (lane >= TOK // 2).astype(i32)
    lanes32 = iota((BAGS, TOK), 1)
    meta = jnp.where(lanes32 == HEAD_DEVS, samples_ref[0:1, 0:1].astype(f32), 0.0)
    for h in range(HEAD_DEVS):
        named = (routes_ref[h : h + 1, :] == bag_row) & (h * FRAMES_DEV + half < count)
        per_bag = jnp.sum(named.astype(f32), axis=1, keepdims=True)
        meta = meta + jnp.where(lanes32 == h, per_bag, 0.0)
    route = routes_ref[pl.ds(head, 1), :]
    live = head * FRAMES_DEV + half < count
    named = ((route == bag_row) & live).astype(f32)
    before = (iota((TOK, TOK), 0) < iota((TOK, TOK), 1)).astype(bf16)
    rank = jnp.sum(named * dot(named.astype(bf16), before), axis=0, keepdims=True)
    target = jnp.where(live, route * MSG + rank.astype(i32), -1000)
    out_row = iota((BAGS * MSG, TOK), 0)
    for q in range(4):
        scatter[:, q * TOK : (q + 1) * TOK] = (out_row == target + CAP * q).astype(f32).astype(bf16)

    sums[...] = jnp.zeros_like(sums)

    def add_taps(slot, a):
        out = slot - a
        frame_id = head * FRAMES_DEV + slot - 1
        scale = jnp.where((frame_id >= 0) & (frame_id < count), 1.0, 0.0)
        cells = (frames[slot].astype(f32) * scale).astype(bf16)
        made = dot(cells, taps[a])
        for e in range(3):
            sums[out, e] += made[:, (3 + e) * COUT : (4 + e) * COUT]
            sums[out, e, 16:CELLS] += made[: CELLS - 16, e * COUT : (e + 1) * COUT]
            sums[out, e, : CELLS - 16] += made[16:, (6 + e) * COUT : (7 + e) * COUT]

    for load in loads:
        load.wait()

    def taps_here(a):
        pltpu.make_async_copy(taps.at[a], taps.at[a], tap_sem.at[a]).wait()

    taps_here(1)
    add_taps(1, 1)
    add_taps(2, 1)
    taps_here(0)
    add_taps(1, 0)
    taps_here(2)
    add_taps(2, 2)

    @pl.when(head > 0)
    def _():
        to_right.wait_recv()

    add_taps(0, 0)

    @pl.when(head < HEAD_DEVS - 1)
    def _():
        to_left.wait_recv()

    add_taps(3, 2)

    column = lax.rem(iota((CELLS, COUT), 0), 16)
    for f in range(FRAMES_DEV):
        scale = jnp.where(head * FRAMES_DEV + f < count, 1.0, 0.0)
        from_left = jnp.where(column == 0, 0.0, pltpu.roll(sums[f, 0], 1, 0))
        from_right = jnp.where(column == 15, 0.0, pltpu.roll(sums[f, 2], CELLS - 1, 0))
        total = (sums[f, 1] + from_left + from_right) * scale
        grid[f * 16 : (f + 1) * 16] = total.reshape(16, 16, COUT)
    quarters = []
    for di in range(2):
        for dj in range(2):
            quarters.extend(grid[2 * r + di, pl.ds(dj, 8, stride=2), :] for r in range(16))
    patches = jnp.concatenate(quarters, axis=0).astype(bf16)

    meta_here = (iota((BAGS * MSG, BAGS), 0) == iota((BAGS * MSG, BAGS), 1) * MSG + 4 * CAP).astype(f32)
    outbox[...] = (dot(scatter[...], patches) + dot(meta_here.astype(bf16), meta.astype(bf16))).astype(bf16)

    def message(ref, at):
        return ref.at[pl.ds(pl.multiple_of(at * MSG, MSG), MSG)]

    own = pltpu.make_async_copy(message(outbox, bag), message(inbox, bag), local_sem.at[0])
    own.start()

    def send(step, carry):
        to = lax.rem(bag + step, BAGS)
        pltpu.make_async_remote_copy(
            src_ref=message(outbox, to),
            dst_ref=message(inbox, bag),
            send_sem=bag_send,
            recv_sem=bag_recv,
            device_id=(to, head),
            device_id_type=MESH,
        ).start()
        return carry

    lax.fori_loop(1, BAGS, send, 0)

    slot = iota((ROWS, BAGS * MSG), 0)
    clip_of = lax.shift_right_logical(slot * 10923, 16)
    wanted = clip_of * MSG + (slot - clip_of * CAP)
    at_col = iota((ROWS, BAGS * MSG), 1)
    for q in range(4):
        unpack[q * ROWS : (q + 1) * ROWS] = (at_col == wanted + q * CAP).astype(f32).astype(bf16)

    own.wait()
    others = inbox.at[pl.ds(0, (BAGS - 1) * MSG)]
    pltpu.make_async_copy(others, others, bag_recv).wait()

    unpacked = dot(unpack[...], inbox[...]).astype(bf16)
    for q in range(4):
        own_rows[:, q * COUT : (q + 1) * COUT] = unpacked[q * ROWS : (q + 1) * ROWS]

    sibling = chip * CORES + 1 - core

    def chunk(of):
        return rows_ref.at[pl.ds(pl.multiple_of(of * ROWS, ROWS), ROWS)]

    def push(source, of, to, sem):
        return pltpu.make_async_remote_copy(
            src_ref=source,
            dst_ref=chunk(of),
            send_sem=head_send.at[sem],
            recv_sem=head_recv.at[of],
            device_id=(bag, to),
            device_id_type=MESH,
        )

    pushes = []
    for step in (2, 1, 3):
        to = lax.rem(chip + step, 4) * CORES + core
        pushes.append(push(own_rows, head, to, step))
    pushes.append(push(own_rows, head, sibling, 0))
    for one in pushes:
        one.start()
    keep = pltpu.make_async_copy(own_rows, chunk(head), local_sem.at[1])
    keep.start()

    pick = (iota((BAGS, BAGS * MSG), 1) == iota((BAGS, BAGS * MSG), 0) * MSG + 4 * CAP).astype(f32)
    told = dot(pick.astype(bf16), inbox[...])
    lane_w = iota((BAGS, COUT), 1)
    counts = jnp.where(lane_w < HEAD_DEVS, told, 0.0)
    clip_total = jnp.sum(counts, axis=1, keepdims=True)
    sample = jnp.sum(jnp.where(lane_w == HEAD_DEVS, told, 0.0), axis=1, keepdims=True)
    row_w = iota((BAGS, COUT), 0)

    def turned(column_of):
        return jnp.sum(jnp.where(row_w == lane_w, column_of, 0.0), axis=0, keepdims=True)

    total_row = turned(clip_total)
    sample_row = turned(sample + 1.0) - 1.0
    same_before = (sample_row == sample) & (lane_w < row_w)
    first = jnp.sum(jnp.where(same_before, total_row, 0.0), axis=1, keepdims=True)
    plan_lane = iota((1, COUT), 1)
    start = jnp.zeros((1, 1), f32)
    by_sample = jnp.zeros((1, COUT), f32)
    for s in range(4):
        first = first + jnp.where(sample == s, start, 0.0)
        size = jnp.sum(jnp.where(sample == s, clip_total, 0.0), axis=0, keepdims=True)
        by_sample = by_sample + jnp.where(plan_lane == s, start, 0.0)
        by_sample = by_sample + jnp.where(plan_lane == 8 + s, size, 0.0)
        start = start + jnp.ceil(size * 0.0625) * 16.0
    plan_row = iota((8, COUT), 0)
    plan = jnp.where(plan_row == 0, turned(first), jnp.where(plan_row == 1, by_sample, 0.0))
    plan_ref[...] = plan.astype(i32)
    slot_of = iota((BAGS, ROWS), 1)
    clip_col = lax.shift_right_logical(slot_of * 10923, 16)
    in_clip = clip_col == iota((BAGS, ROWS), 0)
    slot_row = iota((1, ROWS), 1)
    rank_row = (slot_row - lax.shift_right_logical(slot_row * 10923, 16) * CAP).astype(f32)
    at = first
    for h in range(HEAD_DEVS):
        here = counts[:, h : h + 1]
        at_row = jnp.sum(jnp.where(in_clip, at, 0.0), axis=0, keepdims=True)
        here_row = jnp.sum(jnp.where(in_clip, here, 0.0), axis=0, keepdims=True)
        pos = jnp.where(rank_row < here_row, at_row + rank_row, -1.0)
        pos_ref[h : h + 1, :] = pos.astype(i32)
        at = at + here

    relays = []
    for step in (1, 3, 2):
        of = lax.rem(chip + step, 4) * CORES + core
        pltpu.make_async_copy(chunk(of), chunk(of), head_recv.at[of]).wait()
        relay = push(chunk(of), of, sibling, 3 + step)
        relay.start()
        relays.append(relay)
    for step in range(4):
        of = lax.rem(chip + step, 4) * CORES + 1 - core
        pltpu.make_async_copy(chunk(of), chunk(of), head_recv.at[of]).wait()
    keep.wait()
    for one in pushes + relays:
        one.wait_send()
    sent = outbox.at[pl.ds(0, (BAGS - 1) * MSG)]
    pltpu.make_async_copy(sent, sent, bag_send).wait()

    @pl.when(head < HEAD_DEVS - 1)
    def _():
        to_right.wait_send()

    @pl.when(head > 0)
    def _():
        to_left.wait_send()


def bag_kernel(plan_ref, pos_ref, rows_ref, embed_ref, qkv_ref, out_ref, q_ref, k_ref, v_ref, o_ref):
    v_ref[...] = jnp.zeros_like(v_ref)
    o_ref[...] = jnp.zeros_like(o_ref)
    end = plan_ref[1, 3] + plan_ref[1, 11]

    def project(tile, carry):
        base = pl.multiple_of(tile * TILE, TILE)
        wanted = iota((TILE, ROWS), 0) + base
        picked = jnp.zeros((TILE, CIN), f32)
        for h in range(HEAD_DEVS):
            chosen = (pos_ref[h : h + 1, :] == wanted).astype(f32).astype(bf16)
            picked = picked + dot(chosen, rows_ref[h * ROWS : (h + 1) * ROWS])
        embedded = dot(picked.astype(bf16), embed_ref[...]).astype(bf16).astype(f32)
        scale = lax.rsqrt(jnp.mean(embedded * embedded, axis=-1, keepdims=True) + epsilon)
        normed = (embedded * scale).astype(bf16)
        q_ref[pl.ds(base, TILE)] = (dot(normed, qkv_ref[0]).astype(bf16) * HDIM**-0.5).astype(bf16)
        k_ref[pl.ds(base, TILE)] = dot(normed, qkv_ref[1]).astype(bf16)
        v_ref[pl.ds(base, TILE)] = dot(normed, qkv_ref[2]).astype(bf16)
        return carry

    lax.fori_loop(0, lax.div(end + TILE - 1, TILE), project, 0)

    heads = WIDTH // HDIM
    head_of = lax.shift_right_logical(iota((QTILE, WIDTH), 1), 6)
    key_at = iota((heads * QTILE, TILE), 1)

    for s in range(4):
        start, size = plan_ref[1, s], plan_ref[1, 8 + s]

        def queries(tile, carry, start=start, size=size):
            q0 = pl.multiple_of(start + tile * QTILE, 16)
            block = q_ref[pl.ds(q0, QTILE)].astype(f32)
            spread = jnp.concatenate(
                [jnp.where(head_of == h, block, 0.0) for h in range(heads)], axis=0
            ).astype(bf16)

            def keys(step, state):
                top, norm, total = state
                k0 = pl.multiple_of(start + step * TILE, 16)
                scores = lax.dot_general(
                    spread, k_ref[pl.ds(k0, TILE)], (((1,), (1,)), ((), ())), preferred_element_type=f32
                )
                scores = jnp.where(key_at + step * TILE < size, scores, far_below)
                higher = jnp.maximum(top, jnp.max(scores, axis=-1, keepdims=True))
                shifted = jnp.exp(scores - higher)
                fade = jnp.exp(top - higher)
                norm = norm * fade + jnp.sum(shifted, axis=-1, keepdims=True)
                total = total * fade + dot(shifted.astype(bf16), v_ref[pl.ds(k0, TILE)])
                return higher, norm, total

            state = (
                jnp.full((heads * QTILE, 1), far_below, f32),
                jnp.zeros((heads * QTILE, 1), f32),
                jnp.zeros((heads * QTILE, WIDTH), f32),
            )
            _, norm, total = lax.fori_loop(0, lax.div(size + TILE - 1, TILE), keys, state)
            total = total / norm
            mixed = jnp.zeros((QTILE, WIDTH), f32)
            for h in range(heads):
                mixed = mixed + jnp.where(head_of == h, total[h * QTILE : (h + 1) * QTILE], 0.0)
            o_ref[pl.ds(q0, QTILE)] = mixed
            return carry

        lax.fori_loop(0, lax.div(size + QTILE - 1, QTILE), queries, 0)

    for c in range(BAGS):
        first = plan_ref[0, c]
        over = lax.rem(first, 8)
        block = o_ref[pl.ds(pl.multiple_of(first - over, 8), PER_BAG + 8), :]
        block = pltpu.roll(block, lax.rem(PER_BAG + 8 - over, PER_BAG + 8), 0)
        out_ref[c * PER_BAG : (c + 1) * PER_BAG] = block[:PER_BAG].astype(bf16)


def back_kernel(
    count_ref,
    routes_ref,
    mixed_ref,
    out_ref,
    inbox,
    gather,
    home,
    bag_send,
    bag_recv,
    local_sem,
    head_send,
    head_recv,
):
    bag = lax.axis_index("bag")
    head = lax.axis_index("head")
    count = count_ref[0]
    greet(bag, head)

    def message(ref, at):
        return ref.at[pl.ds(pl.multiple_of(at * PER_BAG, PER_BAG), PER_BAG)]

    own = pltpu.make_async_copy(message(mixed_ref, bag), message(inbox, bag), local_sem.at[0])
    own.start()

    def send(step, carry):
        to = lax.rem(bag + step, BAGS)
        pltpu.make_async_remote_copy(
            src_ref=message(mixed_ref, to),
            dst_ref=message(inbox, bag),
            send_sem=bag_send,
            recv_sem=bag_recv,
            device_id=(to, head),
            device_id_type=MESH,
        ).start()
        return carry

    lax.fori_loop(1, BAGS, send, 0)

    routes_col = jnp.transpose(routes_ref[...])
    half = (iota((TOK, 1), 0) >= TOK // 2).astype(i32)
    before = (iota((TOK, TOK), 1) < iota((TOK, TOK), 0)).astype(bf16)
    at_col = iota((TOK, SLOTS), 1)
    earlier = jnp.zeros((1, TOK), f32)
    for h in range(HEAD_DEVS):
        route = routes_col[:, h : h + 1]
        live = h * FRAMES_DEV + half < count
        named = ((route == iota((TOK, TOK), 1)) & live).astype(f32)
        rank = jnp.sum(named * (dot(before, named.astype(bf16)) + earlier), axis=1, keepdims=True)
        earlier = earlier + jnp.sum(named, axis=0, keepdims=True)
        target = jnp.where(live, route * PER_BAG + rank.astype(i32), -1)
        gather[h * TOK : (h + 1) * TOK] = (at_col == target).astype(f32).astype(bf16)

    own.wait()
    others = inbox.at[pl.ds(0, (BAGS - 1) * PER_BAG)]
    pltpu.make_async_copy(others, others, bag_recv).wait()

    columns = pl.ds(pl.multiple_of(head * WIDTH, WIDTH), WIDTH)

    def deliver(step, carry):
        to = lax.rem(head + step, HEAD_DEVS)
        at = pl.ds(pl.multiple_of(to * TOK, TOK), TOK)
        home[at] = dot(gather[at], inbox[...]).astype(bf16)
        pltpu.make_async_remote_copy(
            src_ref=home.at[at],
            dst_ref=out_ref.at[:, columns],
            send_sem=head_send,
            recv_sem=head_recv,
            device_id=(bag, to),
            device_id_type=MESH,
        ).start()
        return carry

    lax.fori_loop(1, HEAD_DEVS, deliver, 0)
    at = pl.ds(pl.multiple_of(head * TOK, TOK), TOK)
    home[at] = dot(gather[at], inbox[...]).astype(bf16)
    own = pltpu.make_async_copy(home.at[at], out_ref.at[:, columns], local_sem.at[1])
    own.start()
    own.wait()
    arrived = out_ref.at[:, pl.ds(0, (HEAD_DEVS - 1) * WIDTH)]
    pltpu.make_async_copy(arrived, arrived, head_recv).wait()
    left = home.at[pl.ds(0, (HEAD_DEVS - 1) * TOK)]
    pltpu.make_async_copy(left, left, head_send).wait()
    sent = mixed_ref.at[pl.ds(0, (BAGS - 1) * PER_BAG)]
    pltpu.make_async_copy(sent, sent, bag_send).wait()


SMEM = pl.BlockSpec(memory_space=pltpu.SMEM)
VMEM = pl.BlockSpec(memory_space=pltpu.VMEM)
ANY = pl.BlockSpec(memory_space=pl.ANY)


def shards(latents, frame_counts, routes, samples, conv_weight, embed_weight, qkv_weight):
    routes = routes.reshape(HEAD_DEVS, TOK)
    samples = samples.reshape(HEAD_DEVS, TOK)
    latents = latents.reshape(FRAMES_DEV, CELLS, CIN)
    dma, regular = pltpu.SemaphoreType.DMA, pltpu.SemaphoreType.DMA
    rows, pos, plan = pl.pallas_call(
        front_kernel,
        out_shape=(
            jax.ShapeDtypeStruct((SLOTS, CIN), bf16),
            jax.ShapeDtypeStruct((HEAD_DEVS, ROWS), i32),
            jax.ShapeDtypeStruct((8, COUT), i32),
        ),
        in_specs=[SMEM, VMEM, VMEM, ANY, ANY],
        out_specs=(ANY, VMEM, VMEM),
        scratch_shapes=[
            pltpu.VMEM((3, CIN, 9 * COUT), bf16),
            pltpu.VMEM((4, CELLS, CIN), bf16),
            pltpu.VMEM((FRAMES_DEV, 3, CELLS, COUT), f32),
            pltpu.VMEM((FRAMES_DEV * 16, 16, COUT), f32),
            pltpu.VMEM((BAGS * MSG, 4 * TOK), bf16),
            pltpu.VMEM((BAGS * MSG, COUT), bf16),
            pltpu.VMEM((BAGS * MSG, COUT), bf16),
            pltpu.VMEM((4 * ROWS, BAGS * MSG), bf16),
            pltpu.VMEM((ROWS, CIN), bf16),
            dma((FRAMES_DEV,)),
            dma((3,)),
            dma((2,)),
            dma((2,)),
            dma,
            dma,
            dma((2,)),
            dma((7,)),
            dma((HEAD_DEVS,)),
        ],
        compiler_params=pltpu.CompilerParams(
            collective_id=0, has_side_effects=True, vmem_limit_bytes=40 << 20
        ),
        name="front",
    )(frame_counts, routes, samples, latents, conv_weight)
    mixed = pl.pallas_call(
        bag_kernel,
        out_shape=jax.ShapeDtypeStruct((SLOTS, WIDTH), bf16),
        in_specs=[SMEM, VMEM, VMEM, VMEM, VMEM],
        out_specs=VMEM,
        scratch_shapes=[
            pltpu.VMEM((SORTED, WIDTH), bf16),
            pltpu.VMEM((SORTED, WIDTH), bf16),
            pltpu.VMEM((SORTED, WIDTH), bf16),
            pltpu.VMEM((SORTED, WIDTH), f32),
        ],
        compiler_params=pltpu.CompilerParams(vmem_limit_bytes=48 << 20),
        name="bag",
    )(plan, pos, rows, embed_weight, qkv_weight)
    return pl.pallas_call(
        back_kernel,
        out_shape=jax.ShapeDtypeStruct((TOK, D), bf16),
        in_specs=[SMEM, VMEM, ANY],
        out_specs=ANY,
        scratch_shapes=[
            pltpu.VMEM((SLOTS, WIDTH), bf16),
            pltpu.VMEM((HEAD_DEVS * TOK, SLOTS), bf16),
            pltpu.VMEM((HEAD_DEVS * TOK, WIDTH), bf16),
            dma,
            dma,
            dma((2,)),
            dma,
            dma,
        ],
        compiler_params=pltpu.CompilerParams(
            collective_id=1, has_side_effects=True, vmem_limit_bytes=40 << 20
        ),
        name="back",
    )(frame_counts, routes, mixed)


def solution(mesh):
    placed = (
        P("bag", "head", None, None, None),
        P("bag"),
        P("bag", None),
        P("bag"),
        P(),
        P(),
        P(None, None, "head"),
    )
    return jax.shard_map(
        shards, mesh=mesh, in_specs=placed, out_specs=P(("bag", "head"), None), check_vma=False
    )
```

time: 328 us -> 110 us (0.34); the launches traced: 322 us -> 110 us
  Pallas kernels: 0 us -> 104 us
  other arithmetic: 75.9 us -> 0 us
  waiting for transfers between devices: 65.4 us -> 0 us
  matrix products: 56 us -> 0 us
  local copies, waits for them, and re-layouts: 48.6 us -> 5.21 us
  starting transfers between devices: 35.2 us -> 0 us
  blocking collectives: 26.1 us -> 0 us
  between operations: 15.1 us -> 0.71 us
    pallas_call x0 -> x3, Pallas kernels: none -> 104 us  [the longest x1 39.8 us: shards(): pl.pallas_call(front_kernel, out_shape=(jax.ShapeDtypeStruct((SLOTS, CIN)...]
    all_to_all x3 -> x0, waiting for transfers between devices: 65.4 us -> none  [the longest x1 54.1 us: shards(): lax.all_to_all(outgoing, 'bag', split_axis=0, concat_axis=0, tiled=True)]
    dot_general x35 -> x0, matrix products: 56 us -> none  [the longest x3 20 us: attend(): jnp.einsum('hqk,khd->qhd', weights, value_rows, preferred_element_type=jn...]
    sub x3 -> x0, other arithmetic: 47.8 us -> none  [attend(): shifted = jnp.exp(scores - jnp.max(scores, axis=-1, keepdims=True))]
    all_to_all x3 -> x0, starting transfers between devices: 28.1 us -> none  [the longest x1 10.6 us: shards(): lax.all_to_all(slot_labels, 'bag', split_axis=0, concat_axis=0, tiled=True)]
    gather x8 -> x0, local copies, waits for them, and re-layouts: 26.6 us -> none  [the longest x3 9.89 us: shards(): slot_live = filled & token_live.reshape(-1)[flat_index]]
    all_to_all x1 -> x0, blocking collectives: 26.1 us -> none  [shards(): lax.all_to_all(outputs, 'bag', split_axis=0, concat_axis=0, tiled=True)]
    select_n x8 -> x0, other arithmetic: 7.21 us -> none  [the longest x2 3.42 us: shards(): jnp.take(qkv_all, flat_index.reshape(-1), axis=0)]
  transfers between devices with their start and end apart: 6 -> 0, of which waited for: 2 -> 0; matrix products, arithmetic and copies ran while one was open for 18% -> 0% of each run, Pallas kernels for 0% -> 0%
where the time goes in v1:
time: 110 us
  Pallas kernels  104 us (95%)
  local copies, waits for them, and re-layouts  5.21 us (5%)
    pallas_call x1, Pallas kernels, shards(): pl.pallas_call(front_kernel, out_shape=(jax.ShapeDtypeStruct((SLOTS, CIN)...  39.8 us
    pallas_call x1, Pallas kernels, shards(): pl.pallas_call(bag_kernel, out_shape=jax.ShapeDtypeStruct((SLOTS, WIDTH),...  32.4 us
    pallas_call x1, Pallas kernels, shards(): pl.pallas_call(back_kernel, out_shape=jax.ShapeDtypeStruct((TOK, D), bf16...  31.5 us
    unnamed x13, local copies, waits for them, and re-layouts  5.21 us

profile of v1, /device:TPU:1, one launch (start us, length us, event | category | flops | bytes accessed | tf_op | source)
XLA Modules:
  0.0 109.6 jit_solution(9829762336660564197)
XLA Ops:
  0.7 0.0 copy-start
  0.7 2.0 %copy-done = bf16[27,512,128]{2,1,0:T(8,128)(2,1)S(1)} copy-done((bf16[27,512,128]{2,1,0:T(8,128)(2,1)S(1)}, bf16[27,512,128]{2,1,0:T(8,128)(2,1)}, u32[]{:S(2)}) %copy-start) | copy-done | bytes 3538968
  2.7 0.0 copy-start.2
  2.7 1.0 copy-done.2
  3.7 0.0 copy-start.3
  3.7 0.7 copy-done.3
  4.4 0.0 copy-start.5
  4.4 0.7 copy-done.5
  5.1 0.0 copy-start.1
  5.1 39.8 %front.1 = (bf16[1536,512]{1,0:T(8,128)(2,1)S(1)}, s32[8,192]{1,0:T(8,128)S(1)}, s32[8,128]{1,0:T(8,128)S(1)}) custom-call(s32[1]{0:T(128)S(6)} %copy.9.count_ref, s32[8,128]{1,0:T(8,128)S(1)} %bitcast.4, s32[8,128]{1,0:T(8,128)S(1)} %bitcast.6, bf16[2,256,512]{2,1,0:T(8,128)(2,1)S(1)} %bitcast.3, bf16[27,512,128]{2,1,0:T(8,128)(2,1)S(1)} %copy-done), custom_call_target="tpu_custom_call" | custom-call | tf_op jit(solution)/shard_map/front/pallas_call | solution.py:516
  44.8 0.0 copy-done.1
  44.9 0.0 copy-start.4
  44.9 32.4 %bag.1.mixed_ref = bf16[1536,256]{1,0:T(8,128)(2,1)S(1)} custom-call(s32[8,128]{1,0:T(8,128)S(1)} %get-tuple-element.8.plan_ref, s32[8,192]{1,0:T(8,128)S(1)} %get-tuple-element.9.pos_ref, bf16[1536,512]{1,0:T(8,128)(2,1)S(1)} %get-tuple-element.10.rows_ref, bf16[512,2048]{1,0:T(8,128)(2,1)S(1)} %copy-done.1, bf16[3,2048,256]{2,1,0:T(8,128)(2,1)} %qkv_ref.1), custom_call_target="tpu_custom_call" | custom-call | tf_op jit(solution)/shard_map/bag/pallas_call | solution.py:550
  77.3 0.0 copy-done.4
  77.3 31.5 %back.1 = bf16[128,2048]{1,0:T(8,128)(2,1)S(1)} custom-call(s32[1]{0:T(128)S(6)} %copy.9.count_ref, s32[8,128]{1,0:T(8,128)S(1)} %bitcast.5, bf16[1536,256]{1,0:T(8,128)(2,1)S(1)} %bag.1.mixed_ref), custom_call_target="tpu_custom_call" | custom-call | tf_op jit(solution)/shard_map/back/pallas_call | solution.py:564
  108.8 0.8 copy.10
Async XLA Ops:
  0.7 2.0 %copy-start = (bf16[27,512,128]{2,1,0:T(8,128)(2,1)S(1)}, bf16[27,512,128]{2,1,0:T(8,128)(2,1)}, u32[]{:S(2)}) copy-start(bf16[27,512,128]{2,1,0:T(8,128)(2,1)} %conv_ref.1) | copy-start | bytes 10616836
  2.7 1.0 copy-start.2
  3.7 0.7 copy-start.3
  4.4 0.7 copy-start.5
  5.1 39.8 %copy-start.1 = (bf16[512,2048]{1,0:T(8,128)(2,1)S(1)}, bf16[512,2048]{1,0:T(8,128)(2,1)}, u32[]{:S(2)}) copy-start(bf16[512,2048]{1,0:T(8,128)(2,1)} %embed_ref.1) | copy-start | bytes 6291460
  44.9 32.4 %copy-start.4 = (s32[1024,1]{0,1:T(1,128)S(1)}, s32[1024,1]{0,1:T(1,128)}, u32[]{:S(2)}) copy-start(s32[1024,1]{0,1:T(1,128)} %param.9) | copy-start | bytes 12292
